TPU v7x, 256 devices: a whole 4x4x8 slice. The times are simulated.
256 devices in a mesh: dp: 4 (over y), gx: 4 (over x), gy: 16 (over z, core).
Axes of the slice: x: 4, y: 4, z: 8, core: 2. Of those that a mesh axis runs over, the one named last changes fastest.
Arguments:
- field: bfloat16 [4, 64, 32, 20, 2048], P('dp', 'gx', 'gy'), may hold values from -6 to 6
- cotangent: bfloat16 [4, 64, 32, 20, 2048], P('dp', 'gx', 'gy'), may hold values from -6 to 6
- spectral_weight: bfloat16 [24, 24, 20, 20, 192], P(None, None, None, None, ('gx', 'gy')), may hold values from -2.5 to 2.5
- bypass_weight: bfloat16 [20, 20], replicated, may hold values from -1.25 to 1.25
Outputs:
- grad_field: bfloat16 [4, 64, 32, 20, 2048], P('dp', 'gx', 'gy')
- grad_spectral: float32 [24, 24, 20, 20, 192], P(None, None, None, None, ('gx', 'gy'))
- grad_bypass: float32 [20, 20], replicated
All inputs are finite; a program needn't handle non-finite values.
Results may differ from a plain program's by a relative error of at most 0.034.
Values may be sent and summed in bfloat16 or wider, within the bound.
No kernel may reach another device: no remote copies, remote signals or barrier semaphores. Data moves between devices by JAX's collectives and lax.ppermute only.
A program may use at most 192 MiB of HBM per device.

v0:
```python
import math
import jax
import jax.numpy as jnp
from jax import lax
from jax.sharding import PartitionSpec as P

MX = 12
MY = 12
MZ = 12
MT = 4
NZ = 128
NT = 16


def basis(length, kept):
    places = lax.iota(jnp.int32, length)
    orders = lax.iota(jnp.int32, kept)
    cos_arg = places[:, None] * orders[None, :] % length
    sin_arg = places[:, None] * (orders[None, :] + 1) % length
    step_angle = 2.0 * math.pi / length
    scale = math.sqrt(2.0 / length)
    cos_part = jnp.cos(cos_arg.astype(jnp.float32) * step_angle)
    sin_part = jnp.sin(sin_arg.astype(jnp.float32) * step_angle)
    return jnp.concatenate([cos_part, sin_part], axis=1) * scale


def mode_dot(form, data, table):
    upper = table.astype(jnp.bfloat16)
    lower = (table - upper.astype(jnp.float32)).astype(jnp.bfloat16)
    first = jnp.einsum(form, data, upper, preferred_element_type=jnp.float32)
    return first + jnp.einsum(form, data, lower, preferred_element_type=jnp.float32)


def body(field, cotangent, spectral_weight, bypass_weight):
    cells_x = field.shape[1]
    cells_y = field.shape[2]
    channels = field.shape[3]
    parts_x = lax.axis_size("gx")
    parts_y = lax.axis_size("gy")
    table_x = basis(cells_x * parts_x, MX)
    table_y = basis(cells_y * parts_y, MY)
    table_z = basis(NZ, MZ)
    table_t = basis(NT, MT)
    modes_zt = 4 * MZ * MT
    table_zt = (table_z[:, None, :, None] * table_t[None, :, None, :]).reshape(NZ * NT, modes_zt)

    def analyze(cells):
        matrix = cells.reshape(-1, NZ * NT)
        coeff = mode_dot("rp,pq->rq", matrix, table_zt).astype(jnp.bfloat16)
        coeff = coeff.reshape(cells_x, cells_y, channels, modes_zt)
        along_x = lax.all_to_all(coeff, "gx", split_axis=3, concat_axis=0, tiled=True)
        partial_x = mode_dot("xycq,xk->kycq", along_x, table_x).astype(jnp.bfloat16)
        along_y = lax.all_to_all(partial_x, "gy", split_axis=3, concat_axis=1, tiled=True)
        return mode_dot("kycq,yl->klcq", along_y, table_y).astype(jnp.bfloat16)

    def synthesize(spectrum):
        partial_y = mode_dot("klcq,yl->kycq", spectrum, table_y).astype(jnp.bfloat16)
        returned = lax.all_to_all(partial_y, "gy", split_axis=1, concat_axis=3, tiled=True)
        partial_x = mode_dot("kycq,xk->xycq", returned, table_x).astype(jnp.bfloat16)
        coeff = lax.all_to_all(partial_x, "gx", split_axis=0, concat_axis=3, tiled=True)
        matrix = coeff.reshape(-1, modes_zt)
        values = mode_dot("rq,pq->rp", matrix, table_zt)
        return values.reshape(1, cells_x, cells_y, channels, NZ * NT)

    spectrum = analyze(field)
    mixed = jnp.einsum(
        "klcq,klcoq->kloq", spectrum, spectral_weight, preferred_element_type=jnp.float32
    ).astype(jnp.bfloat16)
    spatial = synthesize(mixed)
    bypass = jnp.einsum("bxyip,io->bxyop", field, bypass_weight, preferred_element_type=jnp.float32)
    pre = spatial + bypass
    unused, pullback = jax.vjp(jax.nn.gelu, pre)
    (slope,) = pullback(cotangent.astype(jnp.float32))
    upstream = slope.astype(jnp.bfloat16)
    bypass_term = jnp.einsum("bxyip,bxyop->io", field, upstream, preferred_element_type=jnp.float32)
    grad_bypass = lax.psum(bypass_term, ("dp", "gx", "gy"))
    spectrum_up = analyze(upstream)
    local_grad = jnp.einsum(
        "klcq,kloq->klcoq", spectrum, spectrum_up, preferred_element_type=jnp.float32
    )
    grad_spectral = lax.psum(local_grad.astype(jnp.bfloat16), "dp").astype(jnp.float32)
    spectrum_back = jnp.einsum(
        "kloq,klcoq->klcq", spectrum_up, spectral_weight, preferred_element_type=jnp.float32
    ).astype(jnp.bfloat16)
    through_bypass = jnp.einsum(
        "bxyop,io->bxyip", upstream, bypass_weight, preferred_element_type=jnp.float32
    )
    grad_field = (synthesize(spectrum_back) + through_bypass).astype(jnp.bfloat16)
    return (grad_field, grad_spectral, grad_bypass)


def solution(mesh):
    in_specs = (
        P("dp", "gx", "gy", None, None),
        P("dp", "gx", "gy", None, None),
        P(None, None, None, None, ("gx", "gy")),
        P(),
    )
    out_specs = (P("dp", "gx", "gy", None, None), P(None, None, None, None, ("gx", "gy")), P())
    return jax.shard_map(body, mesh=mesh, in_specs=in_specs, out_specs=out_specs, check_vma=False)
```

profile of v0, /device:TPU:1, one launch (start us, length us, event | category | flops | bytes accessed | tf_op | source)
XLA Modules:
  0.0 493.5 jit_solution(16601009664940160456)
XLA Ops:
  7.5 4.7 copy.145
  12.1 3.6 reshape.139
  15.8 6.2 %fusion = (bf16[128,16,24,8]{1,0,3,2:T(8,128)(2,1)}, bf16[128,16,24,8]{1,0,3,2:T(8,128)(2,1)}) fusion(f32[16,8]{0,1:T(8,128)S(1)} %maximum_multiply_fusion.3, f32[128,24]{0,1:T(8,128)S(1)} %maximum_multiply_fusion.2), kind=kLoop, calls=%fused_computation.5 | loop fusion | flops 1966080 | bytes 1585664 | tf_op jit(solution)/shard_map/convert_element_type | solution.py:29
  22.0 11.6 %convert_element_type.256 = bf16[2048,192]{0,1:T(8,128)(2,1)S(1)} reshape(bf16[128,16,24,8]{1,0,3,2:T(8,128)(2,1)} %get-tuple-element.26) | data formatting | bytes 1572864 | tf_op jit(solution)/shard_map/convert_element_type | solution.py:29
  33.7 12.3 %convert_element_type.253 = bf16[2048,192]{0,1:T(8,128)(2,1)} reshape(bf16[128,16,24,8]{1,0,3,2:T(8,128)(2,1)} %get-tuple-element.27) | data formatting | bytes 1572864 | tf_op jit(solution)/shard_map/convert_element_type | solution.py:28
  46.0 2.2 fusion.114
  48.2 1.8 fusion.30
  49.9 5.9 %reshape.160 = bf16[16,2,20,192]{2,1,0,3:T(2,128)(2,1)S(1)} reshape(bf16[640,192]{0,1:T(8,128)(2,1)} %fusion.30) | data formatting | bytes 491520 | tf_op jit(solution)/shard_map/reshape | solution.py:50
  55.9 4.2 reshape.162
  60.0 4.8 all-to-all-start
  65.0 5.3 %all-to-all-done = bf16[4,2,15360]{2,1,0:T(2,128)(2,1)S(1)} async-done(((bf16[4,2,15360]{2,1,0:T(2,128)(2,1)}), bf16[4,2,15360]{2,1,0:T(2,128)(2,1)S(1)}, u32[]{:S(2)}, u32[]{:S(2)}) %all-to-all-start) | async-done | bytes 245792 | tf_op jit(solution)/shard_map/all_to_all | solution.py:51
  70.3 4.1 reshape.163
  74.4 2.6 copy.218
  78.0 1.3 reshape.164
  79.3 10.9 %all-to-all-start.1 = ((bf16[16,2,1440]{2,1,0:T(2,128)(2,1)}), bf16[16,2,1440]{2,1,0:T(2,128)(2,1)S(1)}, u32[]{:S(2)}, u32[]{:S(2)}) async-start(bf16[16,2,1440]{2,1,0:T(2,128)(2,1)} %reshape.164), calls=%async_computation.1 | async-start | bytes 196608 | tf_op jit(solution)/shard_map/all_to_all | solution.py:53
  90.4 8.2 %all-to-all-done.1 = bf16[16,2,1440]{2,1,0:T(2,128)(2,1)S(1)} async-done(((bf16[16,2,1440]{2,1,0:T(2,128)(2,1)}), bf16[16,2,1440]{2,1,0:T(2,128)(2,1)S(1)}, u32[]{:S(2)}, u32[]{:S(2)}) %all-to-all-start.1) | async-done | bytes 92192 | tf_op jit(solution)/shard_map/all_to_all | solution.py:53
  99.8 1.2 convert_bitcast_fusion
  101.2 5.0 %multiply_reduce_fusion.1 = bf16[24,24,3,20]{1,0,2,3:T(8,128)(2,1)S(1)} fusion(f32[24,24,3,20]{1,0,2,3:T(8,128)S(1)} %copy.223, bf16[24,24,20,20,3]{1,0,4,3,2:T(8,128)(2,1)} %param.6), kind=kLoop, calls=%fused_computation.3 | loop fusion | flops 2039040 | bytes 1589760 | tf_op jit(solution)/shard_map/klcq,klcoq->kloq/dot_general | solution.py:66
  107.7 10.9 %all_to_all.138 = bf16[16,2,1440]{2,1,0:T(2,128)(2,1)S(1)} all-to-all(bf16[16,2,1440]{2,1,0:T(2,128)(2,1)S(1)} %reshape.166), channel_id=1, replica_groups=mesh['dp'=4,'gx'=4,'gy'=16] {'gy'}, dimensions={0} | all-to-all | bytes 184320 | tf_op jit(solution)/shard_map/all_to_all | solution.py:58
  121.2 1.1 reshape.168
  122.3 9.6 %all_to_all.139 = bf16[4,2,15360]{2,1,0:T(2,128)(2,1)S(1)} all-to-all(bf16[4,2,15360]{2,1,0:T(2,128)(2,1)S(1)} %reshape.168), channel_id=1, replica_groups=mesh['dp'=4,'gx'=4,'gy'=16] {'gx'}, dimensions={0} | all-to-all | bytes 491520 | tf_op jit(solution)/shard_map/all_to_all | solution.py:60
  132.7 1.1 copy.164
  133.8 1.5 reshape.141
  135.4 0.8 fusion.118
  136.2 3.3 convolution_add_fusion.1
  139.5 6.7 %reshape.142 = f32[1,16,2,20,2048]{4,3,2,1,0:T(8,128)} reshape(f32[640,2048]{1,0:T(8,128)} %convolution_add_fusion.1) | data formatting | bytes 10485760 | tf_op jit(solution)/shard_map/reshape | solution.py:63
  146.1 11.0 %fusion.4 = bf16[1,16,2,20,2048]{4,3,2,1,0:T(8,128)(2,1)} fusion(f32[1,16,2,20,2048]{4,3,2,1,0:T(8,128)} %reshape.142, bf16[1,16,2,20,2048]{4,2,3,1,0:T(2,128)(2,1)} %param.5, bf16[16,2,20,2048]{3,1,2,0:T(2,128)(2,1)} %bitcast.208, bf16[20,20]{1,0:T(8,128)(2,1)S(1)} %copy-done), kind=kOutput, calls=%fused_computation.13 | convolution fusion | flops 81264640 | bytes 13108000 | tf_op jit(solution)/shard_map/bxyip,io->bxyop/dot_general | solution.py:70
  157.1 5.3 %reshape.144 = bf16[640,2048]{1,0:T(8,128)(2,1)} reshape(bf16[1,16,2,20,2048]{4,3,2,1,0:T(8,128)(2,1)} %fusion.4) | data formatting | bytes 5242880 | tf_op jit(solution)/shard_map/reshape | solution.py:48
  162.4 2.8 fusion.119
  165.2 2.8 fusion.26
  168.0 3.8 reshape.161
  171.8 3.5 reshape.170
  175.3 8.8 %all_to_all.140 = bf16[4,2,15360]{2,1,0:T(2,128)(2,1)} all-to-all(bf16[4,2,15360]{2,1,0:T(2,128)(2,1)S(1)} %reshape.170), channel_id=1, replica_groups=mesh['dp'=4,'gx'=4,'gy'=16] {'gx'}, dimensions={0} | all-to-all | bytes 491520 | tf_op jit(solution)/shard_map/all_to_all | solution.py:51
  184.2 6.0 %reshape.171 = bf16[192,16,2,20]{3,2,1,0:T(2,128)(2,1)S(1)} reshape(bf16[4,2,15360]{2,1,0:T(2,128)(2,1)} %all_to_all.140) | data formatting | bytes 491520
  190.1 3.4 copy.221
  193.6 1.2 copy.170
  195.7 1.3 reshape.172
  196.9 5.2 %all-to-all-start.5 = ((bf16[16,2,1440]{2,1,0:T(2,128)(2,1)}), bf16[16,2,1440]{2,1,0:T(2,128)(2,1)S(1)}, u32[]{:S(2)}, u32[]{:S(2)}) async-start(bf16[16,2,1440]{2,1,0:T(2,128)(2,1)} %reshape.172), calls=%async_computation.5 | async-start | bytes 196608 | tf_op jit(solution)/shard_map/all_to_all | solution.py:53
  202.1 2.2 copy.187
  204.3 6.3 %all-to-all-done.5 = bf16[16,2,1440]{2,1,0:T(2,128)(2,1)S(1)} async-done(((bf16[16,2,1440]{2,1,0:T(2,128)(2,1)}), bf16[16,2,1440]{2,1,0:T(2,128)(2,1)S(1)}, u32[]{:S(2)}, u32[]{:S(2)}) %all-to-all-start.5) | async-done | bytes 92192 | tf_op jit(solution)/shard_map/all_to_all | solution.py:53
  211.7 1.4 convert_bitcast_fusion.1
  213.1 1.4 copy.224
  214.5 5.0 %multiply_reduce_fusion = bf16[24,24,3,20]{1,0,2,3:T(8,128)(2,1)S(1)} fusion(f32[24,24,3,20]{1,0,2,3:T(8,128)S(1)} %copy.224, bf16[24,24,20,20,3]{1,0,4,3,2:T(8,128)(2,1)} %param.6), kind=kLoop, calls=%fused_computation.2 | loop fusion | flops 2039040 | bytes 1589760 | tf_op jit(solution)/shard_map/kloq,klcoq->klcq/dot_general | solution.py:82
  220.4 1.2 reshape.174
  221.6 3.7 all-to-all-start.6
  225.3 4.9 fusion.31
  230.2 76.2 %psum.15 = f32[20,20]{0,1:T(8,128)S(1)} all-reduce(f32[20,20]{0,1:T(8,128)S(1)} %fusion.31), channel_id=1, replica_groups=mesh['dp'=4,'gx'=4,'gy'=16] {'dp','gx','gy'}, use_global_device_ids=true, to_apply=%region_1.2 | all-reduce | flops 400 | bytes 3200 | tf_op jit(solution)/shard_map/psum | solution.py:76
  307.0 2.3 copy.186
  310.3 1.0 copy.181
  311.3 1.3 fusion.122
  312.6 2.1 fusion.19
  314.7 1.4 copy.183
  316.1 1.8 reshape.176
  317.9 3.4 all-to-all-start.7
  321.4 5.3 %fusion.1 = bf16[24,24,20,20,3]{1,0,4,3,2:T(8,128)(2,1)} fusion(f32[24,24,3,20]{1,0,2,3:T(8,128)S(1)} %copy-done.3, f32[24,24,3,20]{1,0,2,3:T(8,128)} %copy.186), kind=kLoop, calls=%fused_computation.10 | loop fusion | flops 1382400 | bytes 1658880 | tf_op jit(solution)/shard_map/convert_element_type | solution.py:81
  327.7 1.1 copy.185
  328.8 1.5 reshape.146
  330.3 0.8 fusion.123
  331.1 3.2 convolution_add_fusion
  334.4 7.2 %reshape.147 = f32[1,16,2,20,2048]{4,3,2,1,0:T(8,128)} reshape(f32[640,2048]{1,0:T(8,128)} %convolution_add_fusion) | data formatting | bytes 10485760 | tf_op jit(solution)/shard_map/reshape | solution.py:63
  341.6 4.1 fusion.12
  345.7 4.2 copy.189
  349.9 126.0 %all-reduce.2.cloned.1.call-done = bf16[24,24,20,20,3]{1,0,4,3,2:T(8,128)(2,1)} async-done(((bf16[24,24,20,20,3]{1,0,4,3,2:T(8,128)(2,1)}), bf16[24,24,20,20,3]{1,0,4,3,2:T(8,128)(2,1)}) %all-reduce.2.cloned.1.call-update) | async-done | bytes 1382416 | tf_op jit(solution)/shard_map/psum | solution.py:81
  475.9 10.2 %convert_element_type.284 = f32[24,24,20,20,3]{1,0,4,3,2:T(8,128)} convert(bf16[24,24,20,20,3]{1,0,4,3,2:T(8,128)(2,1)} %all-reduce.2.cloned.1.call-done) | non-fusion elementwise | flops 691200 | bytes 4147200 | tf_op jit(solution)/shard_map/convert_element_type | solution.py:81
  (58 shorter events, 13.3 us)
Async XLA Ops:
  7.2 139.0 %copy-start = (bf16[20,20]{1,0:T(8,128)(2,1)S(1)}, bf16[20,20]{1,0:T(8,128)(2,1)}, u32[]{:S(2)}) copy-start(bf16[20,20]{1,0:T(8,128)(2,1)} %param.7) | copy-start | bytes 2404
  60.0 10.3 %all-to-all-start = ((bf16[4,2,15360]{2,1,0:T(2,128)(2,1)}), bf16[4,2,15360]{2,1,0:T(2,128)(2,1)S(1)}, u32[]{:S(2)}, u32[]{:S(2)}) async-start(bf16[4,2,15360]{2,1,0:T(2,128)(2,1)} %reshape.162), calls=%async_computation | async-start | bytes 491520 | tf_op jit(solution)/shard_map/all_to_all | solution.py:51
  79.3 19.3 %all-to-all-start.1 = ((bf16[16,2,1440]{2,1,0:T(2,128)(2,1)}), bf16[16,2,1440]{2,1,0:T(2,128)(2,1)S(1)}, u32[]{:S(2)}, u32[]{:S(2)}) async-start(bf16[16,2,1440]{2,1,0:T(2,128)(2,1)} %reshape.164), calls=%async_computation.1 | async-start | bytes 196608 | tf_op jit(solution)/shard_map/all_to_all | solution.py:53
  119.1 16.2 %copy-start.1 = (bf16[2048,192]{0,1:T(8,128)(2,1)S(1)}, bf16[2048,192]{0,1:T(8,128)(2,1)}, u32[]{:S(2)}) copy-start(bf16[2048,192]{0,1:T(8,128)(2,1)} %convert_element_type.253) | copy-start | bytes 2359300
  196.9 13.7 %all-to-all-start.5 = ((bf16[16,2,1440]{2,1,0:T(2,128)(2,1)}), bf16[16,2,1440]{2,1,0:T(2,128)(2,1)S(1)}, u32[]{:S(2)}, u32[]{:S(2)}) async-start(bf16[16,2,1440]{2,1,0:T(2,128)(2,1)} %reshape.172), calls=%async_computation.5 | async-start | bytes 196608 | tf_op jit(solution)/shard_map/all_to_all | solution.py:53
  221.6 87.7 %all-to-all-start.6 = ((bf16[16,2,1440]{2,1,0:T(2,128)(2,1)}), bf16[16,2,1440]{2,1,0:T(2,128)(2,1)S(1)}, u32[]{:S(2)}, u32[]{:S(2)}) async-start(bf16[16,2,1440]{2,1,0:T(2,128)(2,1)} %reshape.174), calls=%async_computation.6 | async-start | bytes 196608 | tf_op jit(solution)/shard_map/all_to_all | solution.py:58
  230.2 91.2 %copy-start.3 = (f32[24,24,3,20]{1,0,2,3:T(8,128)S(1)}, f32[24,24,3,20]{1,0,2,3:T(8,128)}, u32[]{:S(2)}) copy-start(f32[24,24,3,20]{1,0,2,3:T(8,128)} %copy.187) | copy-start | bytes 414724
  317.9 9.0 %all-to-all-start.7 = ((bf16[4,2,15360]{2,1,0:T(2,128)(2,1)}), bf16[4,2,15360]{2,1,0:T(2,128)(2,1)S(1)}, u32[]{:S(2)}, u32[]{:S(2)}) async-start(bf16[4,2,15360]{2,1,0:T(2,128)(2,1)} %reshape.176), calls=%async_computation.7 | async-start | bytes 491520 | tf_op jit(solution)/shard_map/all_to_all | solution.py:60
  321.3 154.6 %all-reduce.2.cloned.1.call-start = ((), (), s32[]{:S(2)}) async-start(), calls=%async_computation.8 | async-start | bytes 14745600 | tf_op jit(solution)/shard_map/psum | solution.py:81
  334.4 7.2 %copy-start.2 = (bf16[1,16,2,20,2048]{4,3,2,1,0:T(8,128)(2,1)S(1)}, bf16[1,16,2,20,2048]{4,3,2,1,0:T(8,128)(2,1)}, u32[]{:S(2)}) copy-start(bf16[1,16,2,20,2048]{4,3,2,1,0:T(8,128)(2,1)} %fusion.4) | copy-start | bytes 7864324
Sparse Core Ops, SparseCore 0:
  326.8 149.0 all-reduce.1
where the time goes:
time: 503 us; the launch traced here: 493 us
  waiting for transfers between devices  146 us (29%)
  local copies, waits for them, and re-layouts  120 us (24%)
  blocking collectives  105 us (21%)
  matrix products  46.5 us (9%)
  other arithmetic  32.3 us (6%)
  starting transfers between devices  28 us (6%)
  between operations  15.1 us (3%)
    psum x1, waiting for transfers between devices, body(): lax.psum(local_grad.astype(jnp.bfloat16), 'dp').astype(jnp.float32)  126 us
    psum x1, blocking collectives, body(): grad_bypass = lax.psum(bypass_term, ('dp', 'gx', 'gy'))  76.2 us
    unnamed x29, local copies, waits for them, and re-layouts  39.6 us
    dot_general x12, matrix products, mode_dot(): jnp.einsum(form, data, lower, preferred_element_type=jnp.float32)  16.9 us
    all_to_all x2, starting transfers between devices, analyze(): lax.all_to_all(partial_x, 'gy', split_axis=3, concat_axis=1, tiled=True)  16.1 us
    all_to_all x2, waiting for transfers between devices, analyze(): lax.all_to_all(partial_x, 'gy', split_axis=3, concat_axis=1, tiled=True)  14.5 us
    reshape x2, local copies, waits for them, and re-layouts, synthesize(): return values.reshape(1, cells_x, cells_y, channels, NZ * NT)  13.9 us
    convert_element_type x1, local copies, waits for them, and re-layouts, mode_dot(): upper = table.astype(jnp.bfloat16)  12.3 us
  transfers between devices with their start and end apart: 6, of which 5 were waited for; matrix products, arithmetic and copies ran while one was open for 8% of the time, Pallas kernels for 0%

commit v1 on v0

--- a/solution.py
+++ b/solution.py
@@ -73,7 +73,7 @@
     (slope,) = pullback(cotangent.astype(jnp.float32))
     upstream = slope.astype(jnp.bfloat16)
     bypass_term = jnp.einsum("bxyip,bxyop->io", field, upstream, preferred_element_type=jnp.float32)
-    grad_bypass = lax.psum(bypass_term, ("dp", "gx", "gy"))
+    grad_bypass = lax.psum(lax.psum(bypass_term, ("gx", "gy")), "dp")
     spectrum_up = analyze(upstream)
     local_grad = jnp.einsum(
         "klcq,kloq->klcoq", spectrum, spectrum_up, preferred_element_type=jnp.float32

time: 503 us -> 688 us (1.37)
  blocking collectives: 105 us -> 287 us
    psum x1 -> x2, blocking collectives: 76.2 us -> 258 us  [body(): grad_bypass = lax.psum(lax.psum(bypass_term, ('gx', 'gy')), 'dp')]
  transfers between devices with their start and end apart: 6 -> 6, of which waited for: 5 -> 4; matrix products, arithmetic and copies ran while one was open for 8% -> 6% of each run, Pallas kernels for 0% -> 0%
where the time goes in v1:
time: 688 us; the launch traced here: 678 us
  blocking collectives  287 us (42%)
  waiting for transfers between devices  149 us (22%)
  local copies, waits for them, and re-layouts  120 us (17%)
  matrix products  46.9 us (7%)
  other arithmetic  32.3 us (5%)
  starting transfers between devices  28 us (4%)
  between operations  15.1 us (2%)
    psum x2, blocking collectives, body(): grad_bypass = lax.psum(lax.psum(bypass_term, ('gx', 'gy')), 'dp')  258 us
    psum x1, waiting for transfers between devices, body(): lax.psum(local_grad.astype(jnp.bfloat16), 'dp').astype(jnp.float32)  129 us
    unnamed x29, local copies, waits for them, and re-layouts  39.6 us
    dot_general x12, matrix products, mode_dot(): jnp.einsum(form, data, lower, preferred_element_type=jnp.float32)  16.8 us
    all_to_all x2, starting transfers between devices, analyze(): lax.all_to_all(partial_x, 'gy', split_axis=3, concat_axis=1, tiled=True)  16.1 us
    all_to_all x2, waiting for transfers between devices, analyze(): lax.all_to_all(partial_x, 'gy', split_axis=3, concat_axis=1, tiled=True)  14.5 us
    reshape x2, local copies, waits for them, and re-layouts, synthesize(): return values.reshape(1, cells_x, cells_y, channels, NZ * NT)  13.9 us
  transfers between devices with their start and end apart: 6, of which 4 were waited for; matrix products, arithmetic and copies ran while one was open for 6% of the time, Pallas kernels for 0%

profile of v1, /device:TPU:1, one launch (start us, length us, event | category | flops | bytes accessed | tf_op | source)
XLA Modules:
  0.0 678.5 jit_solution(7607641703787441757)
XLA Ops:
  7.5 4.7 copy.145
  12.1 3.6 reshape.139
  15.8 6.2 fusion
  22.0 11.6 %convert_element_type.256 = bf16[2048,192]{0,1:T(8,128)(2,1)S(1)} reshape(bf16[128,16,24,8]{1,0,3,2:T(8,128)(2,1)} %get-tuple-element.26) | data formatting | bytes 1572864 | tf_op jit(solution)/shard_map/convert_element_type | solution.py:29
  33.7 12.3 %convert_element_type.253 = bf16[2048,192]{0,1:T(8,128)(2,1)} reshape(bf16[128,16,24,8]{1,0,3,2:T(8,128)(2,1)} %get-tuple-element.27) | data formatting | bytes 1572864 | tf_op jit(solution)/shard_map/convert_element_type | solution.py:28
  46.0 2.2 fusion.114
  48.2 1.8 fusion.30
  49.9 5.9 reshape.160
  55.9 4.2 reshape.162
  60.0 4.8 all-to-all-start
  65.0 5.3 all-to-all-done
  70.3 4.1 reshape.163
  74.4 2.6 copy.218
  78.0 1.3 reshape.164
  79.3 10.9 %all-to-all-start.1 = ((bf16[16,2,1440]{2,1,0:T(2,128)(2,1)}), bf16[16,2,1440]{2,1,0:T(2,128)(2,1)S(1)}, u32[]{:S(2)}, u32[]{:S(2)}) async-start(bf16[16,2,1440]{2,1,0:T(2,128)(2,1)} %reshape.164), calls=%async_computation.1 | async-start | bytes 196608 | tf_op jit(solution)/shard_map/all_to_all | solution.py:53
  90.4 8.2 %all-to-all-done.1 = bf16[16,2,1440]{2,1,0:T(2,128)(2,1)S(1)} async-done(((bf16[16,2,1440]{2,1,0:T(2,128)(2,1)}), bf16[16,2,1440]{2,1,0:T(2,128)(2,1)S(1)}, u32[]{:S(2)}, u32[]{:S(2)}) %all-to-all-start.1) | async-done | bytes 92192 | tf_op jit(solution)/shard_map/all_to_all | solution.py:53
  99.8 1.2 convert_bitcast_fusion
  101.2 5.0 multiply_reduce_fusion.1
  107.7 10.9 %all_to_all.138 = bf16[16,2,1440]{2,1,0:T(2,128)(2,1)S(1)} all-to-all(bf16[16,2,1440]{2,1,0:T(2,128)(2,1)S(1)} %reshape.166), channel_id=1, replica_groups=mesh['dp'=4,'gx'=4,'gy'=16] {'gy'}, dimensions={0} | all-to-all | bytes 184320 | tf_op jit(solution)/shard_map/all_to_all | solution.py:58
  121.2 1.1 reshape.168
  122.3 9.6 %all_to_all.139 = bf16[4,2,15360]{2,1,0:T(2,128)(2,1)S(1)} all-to-all(bf16[4,2,15360]{2,1,0:T(2,128)(2,1)S(1)} %reshape.168), channel_id=1, replica_groups=mesh['dp'=4,'gx'=4,'gy'=16] {'gx'}, dimensions={0} | all-to-all | bytes 491520 | tf_op jit(solution)/shard_map/all_to_all | solution.py:60
  132.7 1.1 copy.164
  133.8 1.5 reshape.141
  136.2 3.2 convolution_add_fusion.1
  139.4 6.7 reshape.142
  146.1 11.0 %fusion.4 = bf16[1,16,2,20,2048]{4,3,2,1,0:T(8,128)(2,1)} fusion(f32[1,16,2,20,2048]{4,3,2,1,0:T(8,128)} %reshape.142, bf16[1,16,2,20,2048]{4,2,3,1,0:T(2,128)(2,1)} %param.5, bf16[16,2,20,2048]{3,1,2,0:T(2,128)(2,1)} %bitcast.208, bf16[20,20]{1,0:T(8,128)(2,1)S(1)} %copy-done), kind=kOutput, calls=%fused_computation.13 | convolution fusion | flops 81264640 | bytes 13108000 | tf_op jit(solution)/shard_map/bxyip,io->bxyop/dot_general | solution.py:70
  157.1 5.3 reshape.144
  162.4 2.8 fusion.119
  165.2 2.8 fusion.26
  168.0 3.8 reshape.161
  171.8 3.5 reshape.170
  175.3 8.9 %all_to_all.140 = bf16[4,2,15360]{2,1,0:T(2,128)(2,1)} all-to-all(bf16[4,2,15360]{2,1,0:T(2,128)(2,1)S(1)} %reshape.170), channel_id=1, replica_groups=mesh['dp'=4,'gx'=4,'gy'=16] {'gx'}, dimensions={0} | all-to-all | bytes 491520 | tf_op jit(solution)/shard_map/all_to_all | solution.py:51
  184.1 6.0 reshape.171
  190.1 3.4 copy.221
  193.5 1.2 copy.170
  195.6 1.3 reshape.172
  196.9 5.1 all-to-all-start.5
  202.0 2.2 copy.187
  204.3 6.3 all-to-all-done.5
  211.7 1.4 convert_bitcast_fusion.1
  213.1 1.4 copy.224
  214.4 5.0 multiply_reduce_fusion
  220.3 1.2 reshape.174
  221.6 3.7 all-to-all-start.6
  225.2 4.9 fusion.31
  230.2 244.2 %psum.22 = f32[20,20]{0,1:T(8,128)S(1)} all-reduce(f32[20,20]{0,1:T(8,128)S(1)} %fusion.31), channel_id=1, replica_groups=mesh['dp'=4,'gx'=4,'gy'=16] {'gx','gy'}, use_global_device_ids=true, to_apply=%region_1.2 | all-reduce | flops 400 | bytes 3200 | tf_op jit(solution)/shard_map/psum | solution.py:76
  474.4 13.6 %psum.23 = f32[20,20]{0,1:T(8,128)S(1)} all-reduce(f32[20,20]{0,1:T(8,128)S(1)} %psum.22), channel_id=1, replica_groups=mesh['dp'=4,'gx'=4,'gy'=16] {'dp'}, use_global_device_ids=true, to_apply=%region_2.3 | all-reduce | flops 400 | bytes 3200 | tf_op jit(solution)/shard_map/psum | solution.py:76
  488.7 2.3 copy.186
  491.9 1.0 copy.181
  492.9 1.3 fusion.122
  494.2 2.1 fusion.19
  496.3 1.4 copy.183
  497.7 1.8 reshape.176
  499.5 3.4 all-to-all-start.7
  503.0 5.3 fusion.1
  509.2 1.1 copy.185
  510.3 1.5 reshape.146
  511.8 0.8 fusion.123
  512.6 3.2 convolution_add_fusion
  515.8 7.2 %reshape.147 = f32[1,16,2,20,2048]{4,3,2,1,0:T(8,128)} reshape(f32[640,2048]{1,0:T(8,128)} %convolution_add_fusion) | data formatting | bytes 10485760 | tf_op jit(solution)/shard_map/reshape | solution.py:63
  523.1 4.5 fusion.12
  527.6 4.2 copy.189
  531.8 129.1 %all-reduce.2.cloned.1.call-done = bf16[24,24,20,20,3]{1,0,4,3,2:T(8,128)(2,1)} async-done(((bf16[24,24,20,20,3]{1,0,4,3,2:T(8,128)(2,1)}), bf16[24,24,20,20,3]{1,0,4,3,2:T(8,128)(2,1)}) %all-reduce.2.cloned.1.call-update) | async-done | bytes 1382416 | tf_op jit(solution)/shard_map/psum | solution.py:81
  660.9 10.2 %convert_element_type.284 = f32[24,24,20,20,3]{1,0,4,3,2:T(8,128)} convert(bf16[24,24,20,20,3]{1,0,4,3,2:T(8,128)(2,1)} %all-reduce.2.cloned.1.call-done) | non-fusion elementwise | flops 691200 | bytes 4147200 | tf_op jit(solution)/shard_map/convert_element_type | solution.py:81
  (59 shorter events, 14.0 us)
Async XLA Ops:
  7.2 139.0 %copy-start = (bf16[20,20]{1,0:T(8,128)(2,1)S(1)}, bf16[20,20]{1,0:T(8,128)(2,1)}, u32[]{:S(2)}) copy-start(bf16[20,20]{1,0:T(8,128)(2,1)} %param.7) | copy-start | bytes 2404
  60.0 10.3 %all-to-all-start = ((bf16[4,2,15360]{2,1,0:T(2,128)(2,1)}), bf16[4,2,15360]{2,1,0:T(2,128)(2,1)S(1)}, u32[]{:S(2)}, u32[]{:S(2)}) async-start(bf16[4,2,15360]{2,1,0:T(2,128)(2,1)} %reshape.162), calls=%async_computation | async-start | bytes 491520 | tf_op jit(solution)/shard_map/all_to_all | solution.py:51
  79.3 19.3 %all-to-all-start.1 = ((bf16[16,2,1440]{2,1,0:T(2,128)(2,1)}), bf16[16,2,1440]{2,1,0:T(2,128)(2,1)S(1)}, u32[]{:S(2)}, u32[]{:S(2)}) async-start(bf16[16,2,1440]{2,1,0:T(2,128)(2,1)} %reshape.164), calls=%async_computation.1 | async-start | bytes 196608 | tf_op jit(solution)/shard_map/all_to_all | solution.py:53
  119.1 16.2 %copy-start.1 = (bf16[2048,192]{0,1:T(8,128)(2,1)S(1)}, bf16[2048,192]{0,1:T(8,128)(2,1)}, u32[]{:S(2)}) copy-start(bf16[2048,192]{0,1:T(8,128)(2,1)} %convert_element_type.253) | copy-start | bytes 2359300
  196.9 13.7 %all-to-all-start.5 = ((bf16[16,2,1440]{2,1,0:T(2,128)(2,1)}), bf16[16,2,1440]{2,1,0:T(2,128)(2,1)S(1)}, u32[]{:S(2)}, u32[]{:S(2)}) async-start(bf16[16,2,1440]{2,1,0:T(2,128)(2,1)} %reshape.172), calls=%async_computation.5 | async-start | bytes 196608 | tf_op jit(solution)/shard_map/all_to_all | solution.py:53
  221.6 269.4 %all-to-all-start.6 = ((bf16[16,2,1440]{2,1,0:T(2,128)(2,1)}), bf16[16,2,1440]{2,1,0:T(2,128)(2,1)S(1)}, u32[]{:S(2)}, u32[]{:S(2)}) async-start(bf16[16,2,1440]{2,1,0:T(2,128)(2,1)} %reshape.174), calls=%async_computation.6 | async-start | bytes 196608 | tf_op jit(solution)/shard_map/all_to_all | solution.py:58
  230.2 272.8 %copy-start.3 = (f32[24,24,3,20]{1,0,2,3:T(8,128)S(1)}, f32[24,24,3,20]{1,0,2,3:T(8,128)}, u32[]{:S(2)}) copy-start(f32[24,24,3,20]{1,0,2,3:T(8,128)} %copy.187) | copy-start | bytes 414724
  499.5 8.8 %all-to-all-start.7 = ((bf16[4,2,15360]{2,1,0:T(2,128)(2,1)}), bf16[4,2,15360]{2,1,0:T(2,128)(2,1)S(1)}, u32[]{:S(2)}, u32[]{:S(2)}) async-start(bf16[4,2,15360]{2,1,0:T(2,128)(2,1)} %reshape.176), calls=%async_computation.7 | async-start | bytes 491520 | tf_op jit(solution)/shard_map/all_to_all | solution.py:60
  502.9 158.0 %all-reduce.2.cloned.1.call-start = ((), (), s32[]{:S(2)}) async-start(), calls=%async_computation.8 | async-start | bytes 14745600 | tf_op jit(solution)/shard_map/psum | solution.py:81
  515.8 7.2 %copy-start.2 = (bf16[1,16,2,20,2048]{4,3,2,1,0:T(8,128)(2,1)S(1)}, bf16[1,16,2,20,2048]{4,3,2,1,0:T(8,128)(2,1)}, u32[]{:S(2)}) copy-start(bf16[1,16,2,20,2048]{4,3,2,1,0:T(8,128)(2,1)} %fusion.4) | copy-start | bytes 7864324
Sparse Core Ops, SparseCore 0:
  508.5 152.4 all-reduce.1
